TPU v7x, 256 devices: a whole 4x4x8 slice. The times are simulated.
256 devices in a mesh: ctx: 32 (over z, y), head: 8 (over x, core).
Axes of the slice: x: 4, y: 4, z: 8, core: 2. Of those that a mesh axis runs over, the one named last changes fastest.
Arguments:
- query: bfloat16 [8192, 4096], P('ctx', 'head'), may hold values from -6 to 6
- key: bfloat16 [8192, 4096], P('ctx', 'head'), may hold values from -6 to 6
- value: bfloat16 [8192, 4096], P('ctx', 'head'), may hold values from -6 to 6
- episode_lengths: int32 [8], replicated, may hold values from 1 to 4096, 8192 in all
- attn_gain: float32 [4096], P('head'), may hold values from 0.1 to 1.9
- out_weight: bfloat16 [4096, 3072], P('head', 'ctx'), may hold values from -0.09375 to 0.09375
- residual: bfloat16 [8192, 3072], P('ctx', 'head'), may hold values from -36 to 36
- norm_gain: float32 [3072], P('head'), may hold values from 0.1 to 1.9
- expert_ids: int32 [8192, 2], P('ctx'), may hold values from 0 to 31, all different within a row; in each aligned block of 256 rows (0 to 255, 256 to 511, ...) at most 24 rows name the same one
- route_weights: int32 [8192, 2], P('ctx'), may hold values from 4096 to 65535
- gate_weight: bfloat16 [32, 3072, 5120], P('ctx', None, 'head'), may hold values from -0.109375 to 0.109375
- up_weight: bfloat16 [32, 3072, 5120], P('ctx', None, 'head'), may hold values from -0.109375 to 0.109375
- down_weight: bfloat16 [32, 5120, 3072], P('ctx', 'head'), may hold values from -0.125 to 0.125
Outputs:
- layer_out: bfloat16 [8192, 3072], P('ctx', 'head')
Inputs may be any that keep to these rules, and one draw needn't show every extreme that they name: `expert_ids`: in the rows of one device (256 tokens) no expert is named by more than 24 rows, a bound that some block reaches; a row names two different experts.
All inputs are finite; a program needn't handle non-finite values.
Results may differ from a plain program's by a relative error of at most 0.012.
Values may be sent and summed in bfloat16 or wider, within the bound.
No kernel may reach another device: no remote copies, remote signals or barrier semaphores. Data moves between devices by JAX's collectives and lax.ppermute only.
A program may use at most 128 MiB of HBM per device.

v0:
```python
import jax
import jax.numpy as jnp
from jax import lax
from jax.sharding import Mesh
from jax.sharding import PartitionSpec as P

HEAD_DIM = 128
CTX = ("ctx_0", "ctx_1")


highest = lax.Precision.HIGHEST


def nothing_yet(value, identity):
    return jax.tree.map(
        lambda a, e: jnp.broadcast_to(jnp.asarray(e, a.dtype), a.shape), value, identity
    )


def prefix_by_axis(value, axes, combine, identity):
    before = start = nothing_yet(value, identity)
    so_far = value
    for axis in reversed(axes):
        length, position = (lax.axis_size(axis), lax.axis_index(axis))
        pieces = jax.tree.map(
            lambda part, kind: lax.all_gather(part.astype(kind), axis),
            so_far,
            (jnp.bfloat16, jnp.bfloat16),
        )
        inside, so_far = (start, start)
        for k in range(length):
            passed = k < position
            so_far = combine(
                so_far, jax.tree.map(lambda part, own: part[k].astype(own.dtype), pieces, value)
            )
            inside = jax.tree.map(lambda new, old: jnp.where(passed, new, old), so_far, inside)
        before = combine(inside, before)
    return before


def whole_of(value, axes, dim):
    for axis in reversed(axes):
        value = lax.all_gather(value, axis, axis=dim, tiled=True)
    return value


def split_up(value, dim, length):
    before, after = (value.shape[:dim], value.shape[dim + 1 :])
    return jnp.moveaxis(value.reshape(*before, length, -1, *after), dim, 0)


def sent_and_summed(value, axis, dim):
    parts = split_up(value, dim, lax.axis_size(axis))
    arrived = lax.all_to_all(parts, axis, split_axis=0, concat_axis=0, tiled=True)
    return arrived.astype(jnp.float32).sum(axis=0)


def sent_to_all(value, axis):
    copies = jnp.broadcast_to(value, (lax.axis_size(axis), *value.shape))
    return lax.all_to_all(copies, axis, split_axis=0, concat_axis=0, tiled=True)


def over_copies(value, axis):
    everything = sent_to_all(value, axis)
    return jnp.sum(everything, axis=0)


def episode_of(positions, lengths):
    starts = jnp.cumsum(lengths) - lengths
    return jnp.sum((starts[None, :] <= positions[:, None]).astype(jnp.int32), axis=1) - 1


def link_states(earlier, latter):
    marker = jnp.maximum(earlier[0], latter[0])
    joined = jnp.where(latter[0][0] > 0.0, latter[1], earlier[1] + latter[1])
    return (marker, joined)


def on_device(
    query,
    key,
    value,
    episode_lengths,
    attn_gain,
    out_weight,
    residual,
    norm_gain,
    expert_ids,
    route_weights,
    gate_weight,
    up_weight,
    down_weight,
):
    tok_rows = query.shape[0]
    head_size = HEAD_DIM
    heads_local = query.shape[1] // head_size
    own_index = lax.axis_index(CTX)
    ctx_count = lax.axis_size(CTX)
    positions = own_index * tok_rows + jnp.arange(tok_rows, dtype=jnp.int32)
    episode = episode_of(positions, episode_lengths)
    prior = episode_of(positions[:1] - 1, episode_lengths)[0]
    final = episode[-1]
    lifted_query = jax.nn.silu(query.astype(jnp.float32)).reshape(tok_rows, heads_local, head_size)
    lifted_key = jax.nn.silu(key.astype(jnp.float32)).reshape(tok_rows, heads_local, head_size)
    value_rows = value.astype(jnp.float32).reshape(tok_rows, heads_local, head_size)
    keep = (episode == final).astype(jnp.float32)
    state = jnp.einsum(
        "shd,she->hde", lifted_key * keep[:, None, None], value_rows, precision=highest
    )
    marker = (final != prior).astype(jnp.float32).reshape(1)
    blank = (jnp.zeros((1,), jnp.float32), jnp.zeros_like(state))
    carried = prefix_by_axis((marker, state), CTX, link_states, blank)
    carry_state = carried[1]
    order = jnp.arange(tok_rows, dtype=jnp.int32)
    allowed = ((order[:, None] >= order[None, :]) & (episode[:, None] == episode[None, :])).astype(
        jnp.float32
    )
    scores = jnp.einsum("thd,shd->hts", lifted_query, lifted_key, precision=highest)
    inside = jnp.einsum("hts,shd->thd", scores * allowed[None], value_rows, precision=highest)
    outside = jnp.einsum("thd,hde->the", lifted_query, carry_state, precision=highest)
    attn = inside + outside * (episode == prior).astype(jnp.float32)[:, None, None]
    mean_square = jnp.mean(attn * attn, axis=2, keepdims=True)
    scaled = attn * lax.rsqrt(mean_square + 1e-06) * attn_gain.reshape(heads_local, head_size)
    headed = scaled.reshape(tok_rows, heads_local * head_size).astype(jnp.bfloat16)
    mixed_part = jnp.dot(headed, whole_of(out_weight, CTX, 1), preferred_element_type=jnp.float32)
    width = mixed_part.shape[1]
    mixed_slice = sent_and_summed(mixed_part.astype(jnp.bfloat16), "head", 1)
    hidden_slice = residual.astype(jnp.float32) + mixed_slice
    squares = over_copies(jnp.sum(hidden_slice * hidden_slice, axis=1), "head")
    normed = (hidden_slice * lax.rsqrt(squares / width + 1e-06)[:, None] * norm_gain).astype(
        jnp.bfloat16
    )
    experts_count = gate_weight.shape[0] * ctx_count
    capacity = 3 * tok_rows // experts_count
    flat_ids = expert_ids.reshape(-1)
    onehot = (flat_ids[:, None] == jnp.arange(experts_count, dtype=jnp.int32)[None, :]).astype(
        jnp.int32
    )
    slot = jnp.sum(jnp.cumsum(onehot, axis=0) * onehot, axis=1) - 1
    source_rows = jnp.repeat(normed, 2, axis=0)
    outgoing = (
        jnp.zeros((experts_count, capacity, normed.shape[1]), jnp.bfloat16)
        .at[flat_ids, slot]
        .set(source_rows)
    )
    raw_weights = route_weights.astype(jnp.float32)
    share = (raw_weights / jnp.sum(raw_weights, axis=1, keepdims=True)).reshape(-1)
    full_rows = lax.all_gather(
        lax.all_to_all(outgoing, CTX, split_axis=0, concat_axis=0, tiled=True),
        "head",
        axis=2,
        tiled=True,
    )
    flat = full_rows.reshape(-1, full_rows.shape[2])
    gate = jnp.dot(flat, gate_weight[0], preferred_element_type=jnp.float32)
    up = jnp.dot(flat, up_weight[0], preferred_element_type=jnp.float32)
    gated = (jax.nn.silu(gate) * up).astype(jnp.bfloat16)
    partial_value = jnp.dot(gated, down_weight[0], preferred_element_type=jnp.float32).astype(
        jnp.bfloat16
    )
    answer_partial_value = partial_value.reshape(
        full_rows.shape[0], full_rows.shape[1], partial_value.shape[1]
    )
    summed = sent_and_summed(
        lax.optimization_barrier(answer_partial_value).astype(jnp.float32).astype(jnp.bfloat16),
        "head",
        2,
    )
    returned = lax.all_to_all(
        summed.astype(jnp.bfloat16), CTX, split_axis=0, concat_axis=0, tiled=True
    ).astype(summed.dtype)
    picked = returned[flat_ids, slot]
    weighted = jnp.sum((picked * share[:, None]).reshape(tok_rows, 2, picked.shape[1]), axis=1)
    return (hidden_slice + weighted).astype(jnp.bfloat16)


def solution(mesh):
    torus = Mesh(mesh.devices.reshape(8, 4, mesh.shape["head"]), ("ctx_0", "ctx_1", "head"))
    in_specs = (
        P(CTX, "head"),
        P(CTX, "head"),
        P(CTX, "head"),
        P(),
        P("head"),
        P("head", CTX),
        P(CTX, "head"),
        P("head"),
        P(CTX, None),
        P(CTX, None),
        P(CTX, None, "head"),
        P(CTX, None, "head"),
        P(CTX, "head", None),
    )
    out_specs = P(CTX, "head")
    return jax.shard_map(
        on_device, mesh=torus, in_specs=in_specs, out_specs=out_specs, check_vma=False
    )
```

profile of v0, /device:TPU:8, one launch (start us, length us, event | category | flops | bytes accessed | tf_op | source)
XLA Modules:
  0.0 374.9 jit_solution(1140005063980959960)
XLA Ops:
  8.6 1.4 fusion.82
  14.0 1.3 dynamic-slice
  16.5 13.7 %all-gather = bf16[16,128,128]{2,1,0:T(8,128)(2,1)S(1)} all-gather(bf16[4,128,128]{2,1,0:T(8,128)(2,1)S(1)} %convolution_convert_fusion.2), channel_id=2, replica_groups=mesh['ctx_0'=8,'ctx_1'=4,'head'=8] {'ctx_1'}, dimensions={0}, use_global_device_ids=true | all-gather | bytes 655360 | tf_op jit(solution)/shard_map/all_gather | solution.py:26
  30.2 9.6 %all-reduce = bf16[4]{0:T(256)(128)(2,1)S(1)} all-reduce(bf16[4]{0:T(256)(128)(2,1)S(1)} %dynamic-update-slice), channel_id=1, replica_groups=mesh['ctx_0'=8,'ctx_1'=4,'head'=8] {'ctx_1'}, use_global_device_ids=true, to_apply=%add | all-reduce | flops 4 | bytes 16
  43.2 12.1 %all_gather.38 = bf16[512,384]{0,1:T(8,128)(2,1)} all-gather(bf16[512,96]{0,1:T(8,128)(2,1)S(1)} %copy-done.2), channel_id=1, replica_groups=mesh['ctx_0'=8,'ctx_1'=4,'head'=8] {'ctx_1'}, dimensions={1}, use_global_device_ids=true | all-gather | bytes 491520 | tf_op jit(solution)/shard_map/all_gather | solution.py:43
  57.9 19.5 %all-reduce.1 = bf16[8]{0:T(256)(128)(2,1)S(1)} all-reduce(bf16[8]{0:T(256)(128)(2,1)S(1)} %dynamic-update-slice.1), channel_id=3, replica_groups=mesh['ctx_0'=8,'ctx_1'=4,'head'=8] {'ctx_0'}, use_global_device_ids=true, to_apply=%add.1 | all-reduce | flops 8 | bytes 32
  86.2 2.6 fusion.8
  89.7 39.1 %all-gather.8.cloned.1.call-done = bf16[512,3072]{0,1:T(8,128)(2,1)} async-done(((bf16[512,384]{0,1:T(8,128)(2,1)}), bf16[512,3072]{0,1:T(8,128)(2,1)}) %all-gather.8.cloned.1.call-update) | async-done | bytes 3145744 | tf_op jit(solution)/shard_map/all_gather | solution.py:43
  128.8 2.9 convolution_convert_fusion.1
  133.1 4.4 %all-to-all-start = ((bf16[8,256,384]{2,1,0:T(8,128)(2,1)}), bf16[8,256,384]{2,1,0:T(8,128)(2,1)S(1)}, u32[]{:S(2)}, u32[]{:S(2)}) async-start(bf16[8,256,384]{2,1,0:T(8,128)(2,1)} %bitcast.180), calls=%async_computation | async-start | bytes 3145728 | tf_op jit(solution)/shard_map/all_to_all | solution.py:54
  139.6 19.4 %all-to-all-done = bf16[8,256,384]{2,1,0:T(8,128)(2,1)S(1)} async-done(((bf16[8,256,384]{2,1,0:T(8,128)(2,1)}), bf16[8,256,384]{2,1,0:T(8,128)(2,1)S(1)}, u32[]{:S(2)}, u32[]{:S(2)}) %all-to-all-start) | async-done | bytes 1572896 | tf_op jit(solution)/shard_map/all_to_all | solution.py:54
  160.0 3.3 all-to-all-start.1
  163.5 5.2 %all-to-all-done.1 = f32[8,1,256]{2,1,0:T(1,128)S(1)} async-done(((f32[8,1,256]{2,1,0:T(1,128)}), f32[8,1,256]{2,1,0:T(1,128)S(1)}, u32[]{:S(2)}, u32[]{:S(2)}) %all-to-all-start.1) | async-done | bytes 8224 | tf_op jit(solution)/shard_map/all_to_all | solution.py:60
  169.2 26.8 %scatter_fusion = bf16[32,24,384]{2,1,0:T(8,128)(2,1)S(1)} fusion(bf16[32,24,384]{2,1,0:T(8,128)(2,1)S(1)} %broadcast_in_dim.9, s32[512]{0:T(512)S(1)} %bitcast.183, bf16[512,384]{1,0:T(8,128)(2,1)S(1)} %reshape.343), kind=kCustom, calls=%fused_computation.1 | custom fusion | bytes 1183744 | tf_op jit(solution)/shard_map/scatter | solution.py:144
  196.0 25.6 %all_to_all.26 = bf16[32,24,384]{2,1,0:T(8,128)(2,1)} all-to-all(bf16[32,24,384]{2,1,0:T(8,128)(2,1)S(1)} %scatter_fusion), channel_id=1, replica_groups=mesh['ctx_0'=8,'ctx_1'=4,'head'=8] {'ctx_0','ctx_1'}, dimensions={0} | all-to-all | bytes 1179648 | tf_op jit(solution)/shard_map/all_to_all | solution.py:149
  221.6 31.8 %all-gather.10.cloned.1.call-done = bf16[32,24,3072]{2,1,0:T(8,128)(2,1)} async-done(((bf16[32,24,384]{2,1,0:T(8,128)(2,1)}), bf16[32,24,3072]{2,1,0:T(8,128)(2,1)}) %all-gather.10.cloned.1.call-update) | async-done | bytes 4718608 | tf_op jit(solution)/shard_map/all_gather | solution.py:148
  253.4 7.0 %fusion.3 = f32[768,640]{1,0:T(8,128)S(1)} fusion(bf16[768,3072]{1,0:T(8,128)(2,1)} %bitcast.194, bf16[1,3072,640]{2,1,0:T(8,128)(2,1)} %param.23), kind=kOutput, calls=%fused_computation.7 | convolution fusion | flops 3019898880 | bytes 10616832 | tf_op jit(solution)/shard_map/dot_general | solution.py:155
  260.4 3.9 %multiply_convert_fusion = bf16[768,640]{1,0:T(8,128)(2,1)S(1)} fusion(f32[768,640]{1,0:T(8,128)S(1)} %fusion.3, bf16[768,3072]{1,0:T(8,128)(2,1)S(1)} %bitcast.195, bf16[1,3072,640]{2,1,0:T(8,128)(2,1)S(1)} %copy-done.8), kind=kOutput, calls=%fused_computation.11 | convolution fusion | flops 3022848000 | bytes 11599872 | tf_op jit(solution)/shard_map/dot_general | solution.py:156
  264.3 4.0 %convolution_convert_fusion = bf16[768,3072]{1,0:T(8,128)(2,1)S(1)} fusion(bf16[768,640]{1,0:T(8,128)(2,1)S(1)} %multiply_convert_fusion, bf16[1,640,3072]{2,1,0:T(8,128)(2,1)S(1)} %copy-done.9), kind=kOutput, calls=%fused_computation.2 | convolution fusion | flops 3022258176 | bytes 9633792 | tf_op jit(solution)/shard_map/dot_general | solution.py:158
  270.8 59.3 %all_to_all.27 = bf16[8,32,24,384]{3,2,1,0:T(8,128)(2,1)} all-to-all(bf16[8,32,24,384]{3,2,1,0:T(8,128)(2,1)S(1)} %copy.84), channel_id=1, replica_groups=mesh['ctx_0'=8,'ctx_1'=4,'head'=8] {'head'}, dimensions={0} | all-to-all | bytes 9437184 | tf_op jit(solution)/shard_map/all_to_all | solution.py:54
  330.1 4.0 %reduce_sum.100 = bf16[32,24,384]{2,1,0:T(8,128)(2,1)} reduce(bf16[8,32,24,384]{3,2,1,0:T(8,128)(2,1)} %all_to_all.27, bf16[]{:T(256)} %constant.92.clone.1), dimensions={0}, to_apply=%region_11.12 | reduce | flops 2064384 | bytes 5308418 | tf_op jit(solution)/shard_map/reduce_sum | solution.py:55
  334.1 10.2 %all-to-all-start.4 = ((bf16[32,24,384]{2,1,0:T(8,128)(2,1)}), bf16[32,24,384]{2,1,0:T(8,128)(2,1)S(1)}, u32[]{:S(2)}, u32[]{:S(2)}) async-start(bf16[32,24,384]{2,1,0:T(8,128)(2,1)} %reduce_sum.100), calls=%async_computation.4 | async-start | bytes 1179648 | tf_op jit(solution)/shard_map/all_to_all | solution.py:169
  344.4 17.7 %all-to-all-done.4 = bf16[32,24,384]{2,1,0:T(8,128)(2,1)S(1)} async-done(((bf16[32,24,384]{2,1,0:T(8,128)(2,1)}), bf16[32,24,384]{2,1,0:T(8,128)(2,1)S(1)}, u32[]{:S(2)}, u32[]{:S(2)}) %all-to-all-start.4) | async-done | bytes 589856 | tf_op jit(solution)/shard_map/all_to_all | solution.py:169
  362.2 4.0 %gather_fusion = f32[512,384]{1,0:T(8,128)S(1)} fusion(f32[32,24,384]{2,1,0:T(8,128)S(1)} %convert_element_type.292, s32[512]{0:T(512)S(1)} %bitcast.182), kind=kCustom, calls=%fused_computation | custom fusion | bytes 1576960 | tf_op jit(solution)/shard_map/gather | solution.py:172
  (87 shorter events, 21.4 us)
Async XLA Ops:
  6.5 8.8 %copy-start = (bf16[256,512]{1,0:T(8,128)(2,1)S(1)}, bf16[256,512]{1,0:T(8,128)(2,1)}, u32[]{:S(2)}) copy-start(bf16[256,512]{1,0:T(8,128)(2,1)} %param.15) | copy-start | bytes 786436
  6.5 50.0 %copy-start.11 = (u32[256]{0:T(256)S(1)}, u32[256]{0:T(256)}, u32[]{:S(2)}) copy-start(u32[256]{0:T(256)} %constant.142) | copy-start | bytes 3076
  6.5 36.7 %copy-start.2 = (bf16[512,96]{0,1:T(8,128)(2,1)S(1)}, bf16[512,96]{0,1:T(8,128)(2,1)}, u32[]{:S(2)}) copy-start(bf16[512,96]{0,1:T(8,128)(2,1)} %param.18) | copy-start | bytes 294916
  6.5 78.5 %copy-start.10 = (bf16[256,512]{1,0:T(8,128)(2,1)S(1)}, bf16[256,512]{1,0:T(8,128)(2,1)}, u32[]{:S(2)}) copy-start(bf16[256,512]{1,0:T(8,128)(2,1)} %param.13) | copy-start | bytes 786436
  6.5 79.6 %all-gather.6.cloned.1.call-start = ((), (), s32[]{:S(2)}) async-start(), calls=%async_computation.5 | async-start | bytes 1179648 | tf_op jit(solution)/shard_map/all_gather | solution.py:26
  43.1 85.7 %all-gather.8.cloned.1.call-start = ((), (), s32[]{:S(2)}) async-start(), calls=%async_computation.6 | async-start | bytes 3538944 | tf_op jit(solution)/shard_map/all_gather | solution.py:43
  86.2 3.3 copy-start.4
  131.7 5.7 %copy-start.5 = (s32[256,2]{0,1:T(2,128)S(1)}, s32[256,2]{0,1:T(2,128)}, u32[]{:S(2)}) copy-start(s32[256,2]{0,1:T(2,128)} %param.21) | copy-start | bytes 6148
  131.8 27.5 %copy-start.1 = (bf16[256,384]{1,0:T(8,128)(2,1)S(1)}, bf16[256,384]{1,0:T(8,128)(2,1)}, u32[]{:S(2)}) copy-start(bf16[256,384]{1,0:T(8,128)(2,1)} %param.19) | copy-start | bytes 589828
  133.1 35.6 %copy-start.6 = (f32[384]{0:T(512)S(1)}, f32[384]{0:T(512)}, u32[]{:S(2)}) copy-start(f32[384]{0:T(512)} %param.20) | copy-start | bytes 4612
  133.1 26.0 %all-to-all-start = ((bf16[8,256,384]{2,1,0:T(8,128)(2,1)}), bf16[8,256,384]{2,1,0:T(8,128)(2,1)S(1)}, u32[]{:S(2)}, u32[]{:S(2)}) async-start(bf16[8,256,384]{2,1,0:T(8,128)(2,1)} %bitcast.180), calls=%async_computation | async-start | bytes 3145728 | tf_op jit(solution)/shard_map/all_to_all | solution.py:54
  160.0 8.6 %all-to-all-start.1 = ((f32[8,1,256]{2,1,0:T(1,128)}), f32[8,1,256]{2,1,0:T(1,128)S(1)}, u32[]{:S(2)}, u32[]{:S(2)}) async-start(f32[8,1,256]{2,1,0:T(1,128)} %broadcast_in_dim.10), calls=%async_computation.1 | async-start | bytes 16384 | tf_op jit(solution)/shard_map/all_to_all | solution.py:60
  163.4 90.0 %all-gather.10.cloned.1.call-start = ((), (), s32[]{:S(2)}) async-start(), calls=%async_computation.7 | async-start | bytes 5308416 | tf_op jit(solution)/shard_map/all_gather | solution.py:148
  253.4 7.0 %copy-start.7 = (bf16[32,24,3072]{2,1,0:T(8,128)(2,1)S(1)}, bf16[32,24,3072]{2,1,0:T(8,128)(2,1)}, u32[]{:S(2)}) copy-start(bf16[32,24,3072]{2,1,0:T(8,128)(2,1)} %all-gather.10.cloned.1.call-done) | copy-start | bytes 14155780
  253.4 7.0 %copy-start.8 = (bf16[1,3072,640]{2,1,0:T(8,128)(2,1)S(1)}, bf16[1,3072,640]{2,1,0:T(8,128)(2,1)}, u32[]{:S(2)}) copy-start(bf16[1,3072,640]{2,1,0:T(8,128)(2,1)} %param.24) | copy-start | bytes 11796484
  260.4 3.9 %copy-start.9 = (bf16[1,640,3072]{2,1,0:T(8,128)(2,1)S(1)}, bf16[1,640,3072]{2,1,0:T(8,128)(2,1)}, u32[]{:S(2)}) copy-start(bf16[1,640,3072]{2,1,0:T(8,128)(2,1)} %param.25) | copy-start | bytes 11796484
  330.1 14.2 %copy-start.3 = (s32[256,2]{0,1:T(2,128)S(1)}, s32[256,2]{0,1:T(2,128)}, u32[]{:S(2)}) copy-start(s32[256,2]{0,1:T(2,128)} %param.22) | copy-start | bytes 6148
  334.1 28.0 %all-to-all-start.4 = ((bf16[32,24,384]{2,1,0:T(8,128)(2,1)}), bf16[32,24,384]{2,1,0:T(8,128)(2,1)S(1)}, u32[]{:S(2)}, u32[]{:S(2)}) async-start(bf16[32,24,384]{2,1,0:T(8,128)(2,1)} %reduce_sum.100), calls=%async_computation.4 | async-start | bytes 1179648 | tf_op jit(solution)/shard_map/all_to_all | solution.py:169
Sparse Core Ops, SparseCore 0:
  43.3 39.8 all-gather.5
  85.0 43.7 all-gather.7
  221.7 31.6 all-gather.9
where the time goes:
time: 376 us; the launch traced here: 375 us
  blocking collectives  140 us (37%)
  waiting for transfers between devices  113 us (30%)
  local copies, waits for them, and re-layouts  42.4 us (11%)
  between operations  24.9 us (7%)
  matrix products  22.6 us (6%)
  starting transfers between devices  18 us (5%)
  other arithmetic  14 us (4%)
    all_to_all x1, blocking collectives, sent_and_summed(): lax.all_to_all(parts, axis, split_axis=0, concat_axis=0, tiled=True)  59.3 us
    all_gather x1, waiting for transfers between devices, whole_of(): value = lax.all_gather(value, axis, axis=dim, tiled=True)  39.1 us
    all_gather x1, waiting for transfers between devices, on_device(): lax.all_gather(lax.all_to_all(outgoing, CTX, split_axis=0, concat_axis=0,...  31.8 us
    unnamed x2, blocking collectives  29.1 us
    scatter x1, local copies, waits for them, and re-layouts, on_device(): outgoing = jnp.zeros((experts_count, capacity, normed.shape[1]), jnp.bflo...  26.8 us
    all_to_all x1, blocking collectives, on_device(): lax.all_to_all(outgoing, CTX, split_axis=0, concat_axis=0, tiled=True)  25.6 us
    all_to_all x1, waiting for transfers between devices, sent_and_summed(): lax.all_to_all(parts, axis, split_axis=0, concat_axis=0, tiled=True)  19.4 us
    all_to_all x1, waiting for transfers between devices, on_device(): lax.all_to_all(summed.astype(jnp.bfloat16), CTX, split_axis=0, concat_axi...  17.7 us
  transfers between devices with their start and end apart: 6, of which 5 were waited for; matrix products, arithmetic and copies ran while one was open for 3% of the time, Pallas kernels for 0%

commit v1 on v0

--- a/solution.py
+++ b/solution.py
@@ -66,7 +66,9 @@
 
 
 def episode_of(positions, lengths):
-    starts = jnp.cumsum(lengths) - lengths
+    count = lengths.shape[0]
+    ahead = jnp.arange(count)[:, None] > jnp.arange(count)[None, :]
+    starts = jnp.sum(jnp.where(ahead, lengths[None, :], 0), axis=1)
     return jnp.sum((starts[None, :] <= positions[:, None]).astype(jnp.int32), axis=1) - 1
 
 
@@ -133,10 +135,9 @@
     experts_count = gate_weight.shape[0] * ctx_count
     capacity = 3 * tok_rows // experts_count
     flat_ids = expert_ids.reshape(-1)
-    onehot = (flat_ids[:, None] == jnp.arange(experts_count, dtype=jnp.int32)[None, :]).astype(
-        jnp.int32
-    )
-    slot = jnp.sum(jnp.cumsum(onehot, axis=0) * onehot, axis=1) - 1
+    pair_order = jnp.arange(flat_ids.shape[0])
+    same = (flat_ids[:, None] == flat_ids[None, :]) & (pair_order[:, None] > pair_order[None, :])
+    slot = jnp.sum(same.astype(jnp.int32), axis=1)
     source_rows = jnp.repeat(normed, 2, axis=0)
     outgoing = (
         jnp.zeros((experts_count, capacity, normed.shape[1]), jnp.bfloat16)

time: 376 us -> 374 us (level)
  transfers between devices with their start and end apart: 6 -> 6, of which waited for: 5 -> 5; matrix products, arithmetic and copies ran while one was open for 3% -> 2% of each run, Pallas kernels for 0% -> 0%
where the time goes in v1:
time: 374 us
  blocking collectives  140 us (37%)
  waiting for transfers between devices  114 us (30%)
  local copies, waits for them, and re-layouts  41.8 us (11%)
  between operations  24.8 us (7%)
  matrix products  22.6 us (6%)
  starting transfers between devices  17.9 us (5%)
  other arithmetic  12.3 us (3%)
    all_to_all x1, blocking collectives, sent_and_summed(): lax.all_to_all(parts, axis, split_axis=0, concat_axis=0, tiled=True)  59.3 us
    all_gather x1, waiting for transfers between devices, whole_of(): value = lax.all_gather(value, axis, axis=dim, tiled=True)  38.6 us
    all_gather x1, waiting for transfers between devices, on_device(): lax.all_gather(lax.all_to_all(outgoing, CTX, split_axis=0, concat_axis=0,...  31.8 us
    unnamed x2, blocking collectives  29.6 us
    scatter x1, local copies, waits for them, and re-layouts, on_device(): outgoing = jnp.zeros((experts_count, capacity, normed.shape[1]), jnp.bflo...  26.7 us
    all_to_all x1, blocking collectives, on_device(): lax.all_to_all(outgoing, CTX, split_axis=0, concat_axis=0, tiled=True)  25.6 us
    all_to_all x1, waiting for transfers between devices, sent_and_summed(): lax.all_to_all(parts, axis, split_axis=0, concat_axis=0, tiled=True)  20.9 us
    all_to_all x1, waiting for transfers between devices, on_device(): lax.all_to_all(summed.astype(jnp.bfloat16), CTX, split_axis=0, concat_axi...  17.7 us
  transfers between devices with their start and end apart: 6, of which 5 were waited for; matrix products, arithmetic and copies ran while one was open for 2% of the time, Pallas kernels for 0%

profile of v1, /device:TPU:8, one launch (start us, length us, event | category | flops | bytes accessed | tf_op | source)
XLA Modules:
  0.0 373.6 jit_solution(1136893205991454708)
XLA Ops:
  11.3 1.3 dynamic-slice
  13.8 9.9 %all-reduce = bf16[4]{0:T(256)(128)(2,1)S(1)} all-reduce(bf16[4]{0:T(256)(128)(2,1)S(1)} %dynamic-update-slice), channel_id=1, replica_groups=mesh['ctx_0'=8,'ctx_1'=4,'head'=8] {'ctx_1'}, use_global_device_ids=true, to_apply=%add | all-reduce | flops 4 | bytes 16
  25.5 12.1 %all-gather = bf16[16,128,128]{2,1,0:T(8,128)(2,1)S(1)} all-gather(bf16[4,128,128]{2,1,0:T(8,128)(2,1)S(1)} %convolution_convert_fusion.2), channel_id=2, replica_groups=mesh['ctx_0'=8,'ctx_1'=4,'head'=8] {'ctx_1'}, dimensions={0}, use_global_device_ids=true | all-gather | bytes 655360 | tf_op jit(solution)/shard_map/all_gather | solution.py:26
  41.0 13.6 %all_gather.38 = bf16[512,384]{0,1:T(8,128)(2,1)} all-gather(bf16[512,96]{0,1:T(8,128)(2,1)S(1)} %copy-done.2), channel_id=1, replica_groups=mesh['ctx_0'=8,'ctx_1'=4,'head'=8] {'ctx_1'}, dimensions={1}, use_global_device_ids=true | all-gather | bytes 491520 | tf_op jit(solution)/shard_map/all_gather | solution.py:43
  57.2 19.6 %all-reduce.1 = bf16[8]{0:T(256)(128)(2,1)S(1)} all-reduce(bf16[8]{0:T(256)(128)(2,1)S(1)} %dynamic-update-slice.1), channel_id=3, replica_groups=mesh['ctx_0'=8,'ctx_1'=4,'head'=8] {'ctx_0'}, use_global_device_ids=true, to_apply=%add.1 | all-reduce | flops 8 | bytes 32
  85.6 2.6 fusion.8
  89.1 38.6 %all-gather.8.cloned.1.call-done = bf16[512,3072]{0,1:T(8,128)(2,1)} async-done(((bf16[512,384]{0,1:T(8,128)(2,1)}), bf16[512,3072]{0,1:T(8,128)(2,1)}) %all-gather.8.cloned.1.call-update) | async-done | bytes 3145744 | tf_op jit(solution)/shard_map/all_gather | solution.py:43
  127.7 2.9 convolution_convert_fusion.1
  130.6 1.3 copy.102
  132.0 4.3 %all-to-all-start = ((bf16[8,256,384]{2,1,0:T(8,128)(2,1)}), bf16[8,256,384]{2,1,0:T(8,128)(2,1)S(1)}, u32[]{:S(2)}, u32[]{:S(2)}) async-start(bf16[8,256,384]{2,1,0:T(8,128)(2,1)} %bitcast.160), calls=%async_computation | async-start | bytes 3145728 | tf_op jit(solution)/shard_map/all_to_all | solution.py:54
  136.9 20.9 %all-to-all-done = bf16[8,256,384]{2,1,0:T(8,128)(2,1)S(1)} async-done(((bf16[8,256,384]{2,1,0:T(8,128)(2,1)}), bf16[8,256,384]{2,1,0:T(8,128)(2,1)S(1)}, u32[]{:S(2)}, u32[]{:S(2)}) %all-to-all-start) | async-done | bytes 1572896 | tf_op jit(solution)/shard_map/all_to_all | solution.py:54
  158.8 3.3 all-to-all-start.1
  162.2 5.2 %all-to-all-done.1 = f32[8,1,256]{2,1,0:T(1,128)S(1)} async-done(((f32[8,1,256]{2,1,0:T(1,128)}), f32[8,1,256]{2,1,0:T(1,128)S(1)}, u32[]{:S(2)}, u32[]{:S(2)}) %all-to-all-start.1) | async-done | bytes 8224 | tf_op jit(solution)/shard_map/all_to_all | solution.py:60
  167.9 26.7 %scatter_fusion = bf16[32,24,384]{2,1,0:T(8,128)(2,1)S(1)} fusion(bf16[32,24,384]{2,1,0:T(8,128)(2,1)S(1)} %broadcast_in_dim.27, s32[512]{0:T(512)S(1)} %bitcast.163, bf16[512,384]{1,0:T(8,128)(2,1)S(1)} %reshape.294), kind=kCustom, calls=%fused_computation.1 | custom fusion | bytes 1183744 | tf_op jit(solution)/shard_map/scatter | solution.py:145
  194.7 25.6 %all_to_all.26 = bf16[32,24,384]{2,1,0:T(8,128)(2,1)} all-to-all(bf16[32,24,384]{2,1,0:T(8,128)(2,1)S(1)} %scatter_fusion), channel_id=1, replica_groups=mesh['ctx_0'=8,'ctx_1'=4,'head'=8] {'ctx_0','ctx_1'}, dimensions={0} | all-to-all | bytes 1179648 | tf_op jit(solution)/shard_map/all_to_all | solution.py:150
  220.3 31.8 %all-gather.10.cloned.1.call-done = bf16[32,24,3072]{2,1,0:T(8,128)(2,1)} async-done(((bf16[32,24,384]{2,1,0:T(8,128)(2,1)}), bf16[32,24,3072]{2,1,0:T(8,128)(2,1)}) %all-gather.10.cloned.1.call-update) | async-done | bytes 4718608 | tf_op jit(solution)/shard_map/all_gather | solution.py:149
  252.1 7.0 %fusion.3 = f32[768,640]{1,0:T(8,128)S(1)} fusion(bf16[768,3072]{1,0:T(8,128)(2,1)} %bitcast.172, bf16[1,3072,640]{2,1,0:T(8,128)(2,1)} %param.23), kind=kOutput, calls=%fused_computation.7 | convolution fusion | flops 3019898880 | bytes 10616832 | tf_op jit(solution)/shard_map/dot_general | solution.py:156
  259.1 3.9 %multiply_convert_fusion = bf16[768,640]{1,0:T(8,128)(2,1)S(1)} fusion(f32[768,640]{1,0:T(8,128)S(1)} %fusion.3, bf16[768,3072]{1,0:T(8,128)(2,1)S(1)} %bitcast.173, bf16[1,3072,640]{2,1,0:T(8,128)(2,1)S(1)} %copy-done.8), kind=kOutput, calls=%fused_computation.11 | convolution fusion | flops 3022848000 | bytes 11599872 | tf_op jit(solution)/shard_map/dot_general | solution.py:157
  263.0 4.0 %convolution_convert_fusion = bf16[768,3072]{1,0:T(8,128)(2,1)S(1)} fusion(bf16[768,640]{1,0:T(8,128)(2,1)S(1)} %multiply_convert_fusion, bf16[1,640,3072]{2,1,0:T(8,128)(2,1)S(1)} %copy-done.9), kind=kOutput, calls=%fused_computation.2 | convolution fusion | flops 3022258176 | bytes 9633792 | tf_op jit(solution)/shard_map/dot_general | solution.py:159
  269.5 59.3 %all_to_all.27 = bf16[8,32,24,384]{3,2,1,0:T(8,128)(2,1)} all-to-all(bf16[8,32,24,384]{3,2,1,0:T(8,128)(2,1)S(1)} %copy.74), channel_id=1, replica_groups=mesh['ctx_0'=8,'ctx_1'=4,'head'=8] {'head'}, dimensions={0} | all-to-all | bytes 9437184 | tf_op jit(solution)/shard_map/all_to_all | solution.py:54
  328.8 4.0 %reduce_sum.117 = bf16[32,24,384]{2,1,0:T(8,128)(2,1)} reduce(bf16[8,32,24,384]{3,2,1,0:T(8,128)(2,1)} %all_to_all.27, bf16[]{:T(256)} %constant.81.clone.1), dimensions={0}, to_apply=%region_9.10 | reduce | flops 2064384 | bytes 5308418 | tf_op jit(solution)/shard_map/reduce_sum | solution.py:55
  332.8 10.2 %all-to-all-start.4 = ((bf16[32,24,384]{2,1,0:T(8,128)(2,1)}), bf16[32,24,384]{2,1,0:T(8,128)(2,1)S(1)}, u32[]{:S(2)}, u32[]{:S(2)}) async-start(bf16[32,24,384]{2,1,0:T(8,128)(2,1)} %reduce_sum.117), calls=%async_computation.4 | async-start | bytes 1179648 | tf_op jit(solution)/shard_map/all_to_all | solution.py:170
  343.2 17.7 %all-to-all-done.4 = bf16[32,24,384]{2,1,0:T(8,128)(2,1)S(1)} async-done(((bf16[32,24,384]{2,1,0:T(8,128)(2,1)}), bf16[32,24,384]{2,1,0:T(8,128)(2,1)S(1)}, u32[]{:S(2)}, u32[]{:S(2)}) %all-to-all-start.4) | async-done | bytes 589856 | tf_op jit(solution)/shard_map/all_to_all | solution.py:170
  360.9 4.0 %gather_fusion = f32[512,384]{1,0:T(8,128)S(1)} fusion(f32[32,24,384]{2,1,0:T(8,128)S(1)} %convert_element_type.292, s32[512]{0:T(512)S(1)} %bitcast.162), kind=kCustom, calls=%fused_computation | custom fusion | bytes 1576960 | tf_op jit(solution)/shard_map/gather | solution.py:173
  (80 shorter events, 19.2 us)
Async XLA Ops:
  6.5 18.5 %copy-start = (bf16[256,512]{1,0:T(8,128)(2,1)S(1)}, bf16[256,512]{1,0:T(8,128)(2,1)}, u32[]{:S(2)}) copy-start(bf16[256,512]{1,0:T(8,128)(2,1)} %param.15) | copy-start | bytes 786436
  6.5 49.3 %copy-start.11 = (u32[256]{0:T(256)S(1)}, u32[256]{0:T(256)}, u32[]{:S(2)}) copy-start(u32[256]{0:T(256)} %constant.131) | copy-start | bytes 3076
  6.5 34.4 %copy-start.2 = (bf16[512,96]{0,1:T(8,128)(2,1)S(1)}, bf16[512,96]{0,1:T(8,128)(2,1)}, u32[]{:S(2)}) copy-start(bf16[512,96]{0,1:T(8,128)(2,1)} %param.18) | copy-start | bytes 294916
  6.5 77.9 %copy-start.10 = (bf16[256,512]{1,0:T(8,128)(2,1)S(1)}, bf16[256,512]{1,0:T(8,128)(2,1)}, u32[]{:S(2)}) copy-start(bf16[256,512]{1,0:T(8,128)(2,1)} %param.13) | copy-start | bytes 786436
  6.5 79.1 %all-gather.6.cloned.1.call-start = ((), (), s32[]{:S(2)}) async-start(), calls=%async_computation.5 | async-start | bytes 1179648 | tf_op jit(solution)/shard_map/all_gather | solution.py:26
  40.9 86.7 %all-gather.8.cloned.1.call-start = ((), (), s32[]{:S(2)}) async-start(), calls=%async_computation.6 | async-start | bytes 3538944 | tf_op jit(solution)/shard_map/all_gather | solution.py:43
  85.6 3.3 copy-start.4
  130.6 5.6 %copy-start.5 = (s32[256,2]{0,1:T(2,128)S(1)}, s32[256,2]{0,1:T(2,128)}, u32[]{:S(2)}) copy-start(s32[256,2]{0,1:T(2,128)} %param.21) | copy-start | bytes 6148
  130.6 27.4 %copy-start.1 = (bf16[256,384]{1,0:T(8,128)(2,1)S(1)}, bf16[256,384]{1,0:T(8,128)(2,1)}, u32[]{:S(2)}) copy-start(bf16[256,384]{1,0:T(8,128)(2,1)} %param.19) | copy-start | bytes 589828
  130.6 36.8 %copy-start.6 = (f32[384]{0:T(512)S(1)}, f32[384]{0:T(512)}, u32[]{:S(2)}) copy-start(f32[384]{0:T(512)} %param.20) | copy-start | bytes 4612
  132.0 25.8 %all-to-all-start = ((bf16[8,256,384]{2,1,0:T(8,128)(2,1)}), bf16[8,256,384]{2,1,0:T(8,128)(2,1)S(1)}, u32[]{:S(2)}, u32[]{:S(2)}) async-start(bf16[8,256,384]{2,1,0:T(8,128)(2,1)} %bitcast.160), calls=%async_computation | async-start | bytes 3145728 | tf_op jit(solution)/shard_map/all_to_all | solution.py:54
  158.8 8.6 %all-to-all-start.1 = ((f32[8,1,256]{2,1,0:T(1,128)}), f32[8,1,256]{2,1,0:T(1,128)S(1)}, u32[]{:S(2)}, u32[]{:S(2)}) async-start(f32[8,1,256]{2,1,0:T(1,128)} %broadcast_in_dim.28), calls=%async_computation.1 | async-start | bytes 16384 | tf_op jit(solution)/shard_map/all_to_all | solution.py:60
  162.1 90.0 %all-gather.10.cloned.1.call-start = ((), (), s32[]{:S(2)}) async-start(), calls=%async_computation.7 | async-start | bytes 5308416 | tf_op jit(solution)/shard_map/all_gather | solution.py:149
  252.1 7.0 %copy-start.7 = (bf16[32,24,3072]{2,1,0:T(8,128)(2,1)S(1)}, bf16[32,24,3072]{2,1,0:T(8,128)(2,1)}, u32[]{:S(2)}) copy-start(bf16[32,24,3072]{2,1,0:T(8,128)(2,1)} %all-gather.10.cloned.1.call-done) | copy-start | bytes 14155780
  252.1 7.0 %copy-start.8 = (bf16[1,3072,640]{2,1,0:T(8,128)(2,1)S(1)}, bf16[1,3072,640]{2,1,0:T(8,128)(2,1)}, u32[]{:S(2)}) copy-start(bf16[1,3072,640]{2,1,0:T(8,128)(2,1)} %param.24) | copy-start | bytes 11796484
  259.1 3.9 %copy-start.9 = (bf16[1,640,3072]{2,1,0:T(8,128)(2,1)S(1)}, bf16[1,640,3072]{2,1,0:T(8,128)(2,1)}, u32[]{:S(2)}) copy-start(bf16[1,640,3072]{2,1,0:T(8,128)(2,1)} %param.25) | copy-start | bytes 11796484
  328.8 14.2 %copy-start.3 = (s32[256,2]{0,1:T(2,128)S(1)}, s32[256,2]{0,1:T(2,128)}, u32[]{:S(2)}) copy-start(s32[256,2]{0,1:T(2,128)} %param.22) | copy-start | bytes 6148
  332.8 28.0 %all-to-all-start.4 = ((bf16[32,24,384]{2,1,0:T(8,128)(2,1)}), bf16[32,24,384]{2,1,0:T(8,128)(2,1)S(1)}, u32[]{:S(2)}, u32[]{:S(2)}) async-start(bf16[32,24,384]{2,1,0:T(8,128)(2,1)} %reduce_sum.117), calls=%async_computation.4 | async-start | bytes 1179648 | tf_op jit(solution)/shard_map/all_to_all | solution.py:170
Sparse Core Ops, SparseCore 0:
  41.0 41.0 all-gather.5
  84.0 43.6 all-gather.7
  220.4 31.6 all-gather.9
